TPU v7x, 256 devices: a whole 4x4x8 slice. The times are simulated.
256 devices in a mesh: gx: 64 (over z, y, x_lo), gy: 4 (over x_hi, core).
Axes of the slice: x: 4 (x_hi: 2, x_lo: 2; x = x_hi * 2 + x_lo), y: 4, z: 8, core: 2. Of those that a mesh axis runs over, the one named last changes fastest.
Arguments:
- traces: float32 [64, 8, 4, 128, 1024], P('gx', 'gy'), may hold values from -6 to 6
- leaf_maps: float32 [64, 8, 512, 512], P('gx', 'gy'), may hold values from -4 to 16, as said below
- decap_mask: int32 [64, 8, 4, 8], P('gx', 'gy'), may hold values 0 or 1
Outputs:
- box_maps: float32 [64, 8, 256, 256], P('gx', 'gy')
- box_loads: float32 [64, 8, 256, 1024], P('gx', 'gy')
Inputs may be any that keep to these rules, and one draw needn't show every extreme that they name: `leaf_maps`: every tile's map is symmetric positive definite.
All inputs are finite; a program needn't handle non-finite values. No bound on the sum of `decap_mask` on one device may be relied on, other than what follows from the above.
Results may differ from a plain program's by a relative error of at most 0.0001.
Values sent between devices are 32-bit elements; how exact they have to be, the bound alone decides.
A program may use at most 64 MiB of HBM per device.

v0:
```python
import jax
import jax.numpy as jnp
from jax import lax
from jax.sharding import PartitionSpec as P

PB = 16
LEVELS = 3


decap_admittance = 2.0


def passed_along(block, axis, distance):
    devices = range(lax.axis_size(axis))
    route = [((i - distance) % len(devices), i) for i in devices]
    return lax.ppermute(block, axis, route)


def from_partner(block, axis, stride):
    count = lax.axis_size(axis)
    route = []
    for low in range(count):
        high = low | 1 << stride
        if high != low and high < count:
            route += [(low, high), (high, low)]
    return lax.ppermute(block, axis, route)


def matprod(left, right):
    return jnp.matmul(left, right, precision=lax.Precision.HIGHEST)


def solve_inter(inter, stacked):
    factor = jnp.linalg.cholesky(inter)
    half = jax.scipy.linalg.solve_triangular(factor, stacked, lower=True)
    return jax.scipy.linalg.solve_triangular(factor, half, lower=True, trans=1)


def merge_boxes(left_map, left_load, right_map, right_load, edge):
    a_ww = left_map[..., :edge, :edge]
    a_we = left_map[..., :edge, edge:]
    a_ew = left_map[..., edge:, :edge]
    a_ee = left_map[..., edge:, edge:]
    b_ww = right_map[..., :edge, :edge]
    b_we = right_map[..., :edge, edge:]
    b_ew = right_map[..., edge:, :edge]
    b_ee = right_map[..., edge:, edge:]
    stacked = jnp.concatenate(
        [a_ew, b_we, left_load[..., edge:, :] + right_load[..., :edge, :]], axis=-1
    )
    solved = solve_inter(a_ee + b_ww, stacked)
    first = solved[..., :edge]
    second = solved[..., edge : 2 * edge]
    third = solved[..., 2 * edge :]
    west = jnp.concatenate([a_ww - matprod(a_we, first), -matprod(a_we, second)], axis=-1)
    east = jnp.concatenate([-matprod(b_ew, first), b_ee - matprod(b_ew, second)], axis=-1)
    west_load = left_load[..., :edge, :] - matprod(a_we, third)
    east_load = right_load[..., edge:, :] - matprod(b_ew, third)
    return (
        jnp.concatenate([west, east], axis=-2),
        jnp.concatenate([west_load, east_load], axis=-2),
    )


def body(traces, leaf_maps, decap_mask):
    edge = traces.shape[3]
    columns = traces.shape[4]
    ports_all = 4 * edge
    lead = traces.shape[:2]
    ports = jnp.repeat(decap_mask.astype(jnp.float32), PB, axis=-1).reshape(lead + (ports_all,))
    maps = leaf_maps + decap_admittance * ports[..., None] * jnp.eye(ports_all, dtype=jnp.float32)
    rows_we = maps[..., : 2 * edge, :]
    from_west = passed_along(traces[:, :, 1], "gx", 1)
    from_east = passed_along(traces[:, :, 0], "gx", -1)
    from_south = passed_along(traces[:, 1, 3], "gy", 1)
    from_north = passed_along(traces[:, 0, 2], "gy", -1)
    south_side = jnp.stack([from_south, traces[:, 0, 3]], axis=1)
    north_side = jnp.stack([traces[:, 1, 2], from_north], axis=1)
    neighbour = jnp.stack([from_west, from_east, south_side, north_side], axis=2)
    averaged = 0.5 * (traces + neighbour)
    box_load = matprod(rows_we, averaged.reshape(lead + (ports_all, columns)))
    box_map = maps[..., : 2 * edge, : 2 * edge]
    gx_index = lax.axis_index("gx")
    for level in range(LEVELS):
        is_left = gx_index >> level & 1 == 0
        other_map, other_load = from_partner((box_map, box_load), "gx", level)
        left_map = jnp.where(is_left, box_map, other_map)
        right_map = jnp.where(is_left, other_map, box_map)
        left_load = jnp.where(is_left, box_load, other_load)
        right_load = jnp.where(is_left, other_load, box_load)
        box_map, box_load = merge_boxes(left_map, left_load, right_map, right_load, edge)
    return (box_map, box_load)


def solution(mesh):
    placed = (P("gx", "gy", None, None, None), P("gx", "gy", None, None), P("gx", "gy", None, None))
    return jax.shard_map(
        body,
        mesh=mesh,
        in_specs=placed,
        out_specs=(P("gx", "gy", None, None), P("gx", "gy", None, None)),
        check_vma=False,
    )
```

profile of v0, /device:TPU:8, one launch (start us, length us, event | category | flops | bytes accessed | tf_op | source)
XLA Modules:
  0.0 437.2 jit_solution(8526932472561136313)
XLA Ops:
  0.6 3.3 slice_bitcast_fusion.6
  3.9 1.4 collective-permute-start.2
  5.3 0.6 collective-permute-start.1
  6.0 1.4 slice_bitcast_fusion.28
  7.4 1.9 collective-permute-start.4
  9.4 1.8 copy.106
  11.4 2.1 multiply_add_fusion
  13.5 48.3 %collective-permute-done.4 = f32[1,128,1024]{2,1,0:T(8,128)} collective-permute-done((f32[1,128,1024]{2,1,0:T(8,128)}, f32[1,128,1024]{2,1,0:T(8,128)}, u32[]{:S(2)}, u32[]{:S(2)}) %collective-permute-start.4) | collective-permute-done | bytes 524320 | tf_op jit(solution)/shard_map/ppermute | solution.py:16
  61.7 1.3 maximum_bitcast_fusion.7
  63.0 0.7 collective-permute-done.3
  63.8 1.1 maximum_bitcast_fusion.6
  64.9 2.7 fusion
  67.7 5.0 %convolution_bitcast_fusion.3 = f32[1,2,256,1024]{3,2,1,0:T(8,128)} fusion(f32[2,512,1024]{2,1,0:T(8,128)S(1)} %bitcast.251, f32[1,2,512,512]{2,3,1,0:T(8,128)S(1)} %multiply_add_fusion), kind=kOutput, calls=%fused_computation.9 | convolution fusion | flops 3221225472 | bytes 7340032 | tf_op jit(solution)/shard_map/dot_general | solution.py:30
  73.1 1.8 collective-permute-start
  74.9 56.4 %collective-permute-done = f32[1,2,256,256]{2,3,1,0:T(8,128)} collective-permute-done((f32[1,2,256,256]{2,3,1,0:T(8,128)S(1)}, f32[1,2,256,256]{2,3,1,0:T(8,128)}, u32[]{:S(2)}, u32[]{:S(2)}) %collective-permute-start) | collective-permute-done | bytes 524320 | tf_op jit(solution)/shard_map/ppermute | solution.py:26
  131.3 1.1 broadcast_select_fusion.7
  132.8 23.7 %custom-call.15 = f32[1,2,128,128]{3,2,1,0:T(8,128)S(1)} custom-call(f32[1,2,128,128]{3,2,1,0:T(8,128)S(1)} %fusion.31), custom_call_target="Cholesky" | custom-call | tf_op jit(solution)/shard_map/jit(cholesky)/cholesky | solution.py:34
  156.8 19.7 %custom-call.17 = f32[2,1,128,128]{2,3,1,0:T(8,128)S(1)} custom-call(f32[2,1,128,128]{3,2,1,0:T(8,128)S(1)} %select_bitcast_fusion.2), custom_call_target="InvertDiagBlocksLowerTriangular" | custom-call | tf_op jit(solution)/shard_map/jit(_solve_triangular)/vmap()/triangular_solve | solution.py:36
  176.5 2.7 broadcast_select_fusion.5
  179.3 1.3 fusion.1
  180.6 1.2 convolution_bitcast_fusion.2
  181.8 0.4 slice_subtract_fusion.10
  182.2 0.4 fusion.20
  182.6 1.1 slice_subtract_fusion.4
  183.7 1.1 slice_subtract_fusion.5
  184.8 1.5 pad_maximum_fusion
  186.2 5.9 %collective-permute-start.7 = (f32[1,2,256,1024]{3,2,1,0:T(8,128)}, f32[1,2,256,1024]{3,2,1,0:T(8,128)}, u32[]{:S(2)}, u32[]{:S(2)}) collective-permute-start(f32[1,2,256,1024]{3,2,1,0:T(8,128)} %pad_maximum_fusion), channel_id=1, source_target_pairs={{0,8},{8,0},{4,12},{12,4},{16,24},{24,16},{20,28},{28,20},{32,40},... | collective-permute-start | bytes 6291464 | tf_op jit(solution)/shard_map/ppermute | solution.py:26
  192.5 0.4 slice_subtract_fusion.11
  193.1 0.5 copy-done.6
  193.6 56.2 %collective-permute-done.6 = f32[1,2,256,256]{2,3,1,0:T(8,128)} collective-permute-done((f32[1,2,256,256]{2,3,1,0:T(8,128)S(1)}, f32[1,2,256,256]{2,3,1,0:T(8,128)}, u32[]{:S(2)}, u32[]{:S(2)}) %collective-permute-start.6) | collective-permute-done | bytes 524320 | tf_op jit(solution)/shard_map/ppermute | solution.py:26
  249.8 1.2 broadcast_select_fusion.9
  251.0 0.8 copy.128
  252.0 0.7 fusion.28
  252.7 32.9 %custom-call.18 = f32[1,2,128,128]{3,2,1,0:T(8,128)S(1)} custom-call(f32[1,2,128,128]{3,2,1,0:T(8,128)} %fusion.28), custom_call_target="Cholesky" | custom-call | tf_op jit(solution)/shard_map/jit(cholesky)/cholesky | solution.py:34
  285.6 0.8 select_reduce_fusion.1
  286.5 19.7 %custom-call.20 = f32[2,1,128,128]{2,3,1,0:T(8,128)S(1)} custom-call(f32[2,1,128,128]{3,2,1,0:T(8,128)S(1)} %select_bitcast_fusion.1), custom_call_target="InvertDiagBlocksLowerTriangular" | custom-call | tf_op jit(solution)/shard_map/jit(_solve_triangular)/vmap()/triangular_solve | solution.py:36
  306.2 2.2 broadcast_select_fusion.3
  308.6 0.7 copy-done.8
  309.4 1.3 fusion.6
  310.6 1.2 convolution_bitcast_fusion.1
  311.9 0.4 slice_subtract_fusion.8
  312.3 0.4 fusion.18
  312.7 1.1 slice_subtract_fusion.2
  313.7 1.1 slice_subtract_fusion.3
  314.8 1.5 pad_maximum_fusion.1
  316.5 0.4 fusion.19
  316.9 0.4 slice_subtract_fusion.9
  317.3 3.6 collective-permute-start.8
  320.9 56.0 %collective-permute-done.8 = f32[1,2,256,256]{2,3,1,0:T(8,128)} collective-permute-done((f32[1,2,256,256]{2,3,1,0:T(8,128)S(1)}, f32[1,2,256,256]{2,3,1,0:T(8,128)}, u32[]{:S(2)}, u32[]{:S(2)}) %collective-permute-start.8) | collective-permute-done | bytes 524320 | tf_op jit(solution)/shard_map/ppermute | solution.py:26
  376.9 1.2 broadcast_select_fusion.11
  378.1 0.8 copy.143
  379.1 0.7 fusion.25
  379.7 24.3 %custom-call.21 = f32[1,2,128,128]{3,2,1,0:T(8,128)S(1)} custom-call(f32[1,2,128,128]{3,2,1,0:T(8,128)} %fusion.25), custom_call_target="Cholesky" | custom-call | tf_op jit(solution)/shard_map/jit(cholesky)/cholesky | solution.py:34
  404.0 0.8 select_reduce_fusion
  405.0 19.9 %custom-call.23 = f32[2,1,128,128]{2,3,1,0:T(8,128)S(1)} custom-call(f32[2,1,128,128]{3,2,1,0:T(8,128)S(1)} %select_bitcast_fusion), custom_call_target="InvertDiagBlocksLowerTriangular" | custom-call | tf_op jit(solution)/shard_map/jit(_solve_triangular)/vmap()/triangular_solve | solution.py:36
  424.9 2.2 broadcast_select_fusion.1
  427.3 0.7 copy-done.7
  428.0 1.3 fusion.11
  429.3 1.2 convolution_bitcast_fusion
  431.3 0.4 fusion.17
  432.1 1.1 slice_subtract_fusion
  433.2 1.1 slice_subtract_fusion.1
  434.3 1.0 copy.155
  435.3 1.5 pad_maximum_fusion.2
  (63 shorter events, 4.6 us)
Async XLA Ops:
  0.6 5.3 %copy-start = (f32[1,2,4,128,1024]{4,3,2,1,0:T(8,128)S(1)}, f32[1,2,4,128,1024]{4,3,2,1,0:T(8,128)}, u32[]{:S(2)}) copy-start(f32[1,2,4,128,1024]{4,3,2,1,0:T(8,128)} %param.8) | copy-start | bytes 12582916
  3.9 61.0 %collective-permute-start.2 = (f32[1,2,128,1024]{3,2,1,0:T(8,128)}, f32[1,2,128,1024]{3,2,1,0:T(8,128)}, u32[]{:S(2)}, u32[]{:S(2)}) collective-permute-start(f32[1,2,128,1024]{3,2,1,0:T(8,128)} %get-tuple-element.18), channel_id=1, source_target_pairs={{4,0},{8,4},{12,8},{16,12},{20,16},{24,20},{28,24},{32,28},{36,32}... | collective-permute-start | bytes 3145736 | tf_op jit(solution)/shard_map/ppermute | solution.py:16
  5.3 4.0 copy-start.10
  5.3 4.1 copy-start.2
  5.3 59.6 %collective-permute-start.1 = (f32[1,2,128,1024]{3,2,1,0:T(8,128)}, f32[1,2,128,1024]{3,2,1,0:T(8,128)}, u32[]{:S(2)}, u32[]{:S(2)}) collective-permute-start(f32[1,2,128,1024]{3,2,1,0:T(8,128)} %get-tuple-element.17), channel_id=1, source_target_pairs={{252,0},{0,4},{4,8},{8,12},{12,16},{16,20},{20,24},{24,28},{28,32}... | collective-permute-start | bytes 3145736 | tf_op jit(solution)/shard_map/ppermute | solution.py:16
  7.4 54.4 %collective-permute-start.4 = (f32[1,128,1024]{2,1,0:T(8,128)}, f32[1,128,1024]{2,1,0:T(8,128)}, u32[]{:S(2)}, u32[]{:S(2)}) collective-permute-start(f32[1,128,1024]{2,1,0:T(8,128)} %get-tuple-element.22), channel_id=1, source_target_pairs={{1,0},{2,1},{3,2},{0,3},{5,4},{6,5},{7,6},{4,7},{9,8},{10,9},{11,1... | collective-permute-start | bytes 1572872 | tf_op jit(solution)/shard_map/ppermute | solution.py:16
  9.3 54.5 %collective-permute-start.3 = (f32[1,128,1024]{2,1,0:T(8,128)}, f32[1,128,1024]{2,1,0:T(8,128)}, u32[]{:S(2)}, u32[]{:S(2)}) collective-permute-start(f32[1,128,1024]{2,1,0:T(8,128)} %get-tuple-element.19), channel_id=1, source_target_pairs={{3,0},{0,1},{1,2},{2,3},{7,4},{4,5},{5,6},{6,7},{11,8},{8,9},{9,10... | collective-permute-start | bytes 1572872 | tf_op jit(solution)/shard_map/ppermute | solution.py:16
  11.4 50.4 %copy-start.4 = (f32[1,1,128,1024]{3,2,1,0:T(8,128)S(1)}, f32[1,1,128,1024]{3,2,1,0:T(8,128)}, u32[]{:S(2)}) copy-start(f32[1,1,128,1024]{3,2,1,0:T(8,128)} %get-tuple-element.21) | copy-start | bytes 1572868
  11.4 52.4 %copy-start.3 = (f32[1,1,128,1024]{3,2,1,0:T(8,128)S(1)}, f32[1,1,128,1024]{3,2,1,0:T(8,128)}, u32[]{:S(2)}) copy-start(f32[1,1,128,1024]{3,2,1,0:T(8,128)} %get-tuple-element.20) | copy-start | bytes 1572868
  61.7 3.2 copy-start.1
  72.7 103.8 %collective-permute-start.5 = (f32[1,2,256,1024]{3,2,1,0:T(8,128)}, f32[1,2,256,1024]{3,2,1,0:T(8,128)}, u32[]{:S(2)}, u32[]{:S(2)}) collective-permute-start(f32[1,2,256,1024]{3,2,1,0:T(8,128)} %convolution_bitcast_fusion.3), channel_id=1, source_target_pairs={{0,4},{4,0},{8,12},{12,8},{16,20},{20,16},{24,28},{28,24},{32,36},... | collective-permute-start | bytes 6291464 | tf_op jit(solution)/shard_map/ppermute | solution.py:26
  73.1 58.2 %collective-permute-start = (f32[1,2,256,256]{2,3,1,0:T(8,128)S(1)}, f32[1,2,256,256]{2,3,1,0:T(8,128)}, u32[]{:S(2)}, u32[]{:S(2)}) collective-permute-start(f32[1,2,256,256]{2,3,1,0:T(8,128)S(1)} %slice.224), channel_id=1, source_target_pairs={{0,4},{4,0},{8,12},{12,8},{16,20},{20,16},{24,28},{28,24},{32,36},... | collective-permute-start | bytes 1572872 | tf_op jit(solution)/shard_map/ppermute | solution.py:26
  74.9 104.3 %copy-start.9 = (pred[128,128]{1,0:T(8,128)(4,1)}, pred[128,128]{1,0:T(8,128)(4,1)S(1)}, u32[]{:S(2)}) copy-start(pred[128,128]{1,0:T(8,128)(4,1)S(1)} %iota_compare_fusion.2) | copy-start | bytes 49156
  186.2 120.0 %collective-permute-start.7 = (f32[1,2,256,1024]{3,2,1,0:T(8,128)}, f32[1,2,256,1024]{3,2,1,0:T(8,128)}, u32[]{:S(2)}, u32[]{:S(2)}) collective-permute-start(f32[1,2,256,1024]{3,2,1,0:T(8,128)} %pad_maximum_fusion), channel_id=1, source_target_pairs={{0,8},{8,0},{4,12},{12,4},{16,24},{24,16},{20,28},{28,20},{32,40},... | collective-permute-start | bytes 6291464 | tf_op jit(solution)/shard_map/ppermute | solution.py:26
  192.9 0.7 copy-start.6
  193.0 56.8 %collective-permute-start.6 = (f32[1,2,256,256]{2,3,1,0:T(8,128)S(1)}, f32[1,2,256,256]{2,3,1,0:T(8,128)}, u32[]{:S(2)}, u32[]{:S(2)}) collective-permute-start(f32[1,2,256,256]{2,3,1,0:T(8,128)S(1)} %maximum_maximum_fusion), channel_id=1, source_target_pairs={{0,8},{8,0},{4,12},{12,4},{16,24},{24,16},{20,28},{28,20},{32,40},... | collective-permute-start | bytes 1572872 | tf_op jit(solution)/shard_map/ppermute | solution.py:26
  308.5 0.9 copy-start.8
  316.3 108.6 %collective-permute-start.9 = (f32[1,2,256,1024]{3,2,1,0:T(8,128)}, f32[1,2,256,1024]{3,2,1,0:T(8,128)}, u32[]{:S(2)}, u32[]{:S(2)}) collective-permute-start(f32[1,2,256,1024]{3,2,1,0:T(8,128)} %pad_maximum_fusion.1), channel_id=1, source_target_pairs={{0,16},{16,0},{4,20},{20,4},{8,24},{24,8},{12,28},{28,12},{32,48},... | collective-permute-start | bytes 6291464 | tf_op jit(solution)/shard_map/ppermute | solution.py:26
  317.3 3.7 copy-start.5
  317.3 59.6 %collective-permute-start.8 = (f32[1,2,256,256]{2,3,1,0:T(8,128)S(1)}, f32[1,2,256,256]{2,3,1,0:T(8,128)}, u32[]{:S(2)}, u32[]{:S(2)}) collective-permute-start(f32[1,2,256,256]{2,3,1,0:T(8,128)S(1)} %maximum_maximum_fusion.1), channel_id=1, source_target_pairs={{0,16},{16,0},{4,20},{20,4},{8,24},{24,8},{12,28},{28,12},{32,48},... | collective-permute-start | bytes 1572872 | tf_op jit(solution)/shard_map/ppermute | solution.py:26
  427.1 0.9 copy-start.7
where the time goes:
time: 446 us; the launch traced here: 437 us
  waiting for transfers between devices  218 us (49%)
  other arithmetic  167 us (37%)
  matrix products  23.5 us (5%)
  starting transfers between devices  15.9 us (4%)
  local copies, waits for them, and re-layouts  11.9 us (3%)
    ppermute x6, waiting for transfers between devices, from_partner(): return lax.ppermute(block, axis, route)  169 us
    another operation x10, other arithmetic, solve_inter(): factor = jnp.linalg.cholesky(inter)  82.8 us
    another operation x7, other arithmetic, solve_inter(): return jax.scipy.linalg.solve_triangular(factor, half, lower=True, trans=1)  59.6 us
    ppermute x4, waiting for transfers between devices, passed_along(): return lax.ppermute(block, axis, route)  49 us
    dot_general x19, matrix products, matprod(): return jnp.matmul(left, right, precision=lax.Precision.HIGHEST)  16.1 us
    ppermute x6, starting transfers between devices, from_partner(): return lax.ppermute(block, axis, route)  11.9 us
  transfers between devices with their start and end apart: 10, of which 5 were waited for; matrix products, arithmetic and copies ran while one was open for 36% of the time, Pallas kernels for 0%

commit v1 on v0

v1 whole, which is shorter than its diff:
```python
import functools

import jax
import jax.numpy as jnp
from jax import lax
from jax.experimental import pallas as pl
from jax.experimental.pallas import tpu as pltpu
from jax.sharding import PartitionSpec as P

E = 128
K = 1024
PB = 16
F32 = jnp.float32
BF16 = jnp.bfloat16
NB = 32
MESH = pl.DeviceIdType.MESH

decap_admittance = 2.0


def exact(left, right):
    return jnp.dot(left, right, precision=lax.Precision.HIGHEST, preferred_element_type=F32)


def halves(a):
    high = a.astype(BF16)
    return high, (a - high.astype(F32)).astype(BF16)


def split_dot(left, right):
    lh, ll = left
    rh, rl = right
    dot = functools.partial(jnp.dot, preferred_element_type=F32)
    return dot(lh, rl) + dot(ll, rh) + dot(lh, rh)


def near(left, right):
    return split_dot(halves(left), halves(right))


def invert_blocks(blocks):
    n = blocks[0].shape[0]
    lane = lax.broadcasted_iota(jnp.int32, (n, n), 1)
    row = lax.broadcasted_iota(jnp.int32, (n, n), 0)
    lane8 = lane[:8]
    for k in range(0, n, 2):
        done = []
        for a in blocks:
            c0 = jnp.broadcast_to(a[:, k : k + 1], (n, n))
            c1 = jnp.broadcast_to(a[:, k + 1 : k + 2], (n, n))

            def spread(v, i):
                return jnp.broadcast_to(v[i : i + 1, :], (8, n))

            inv0 = 1.0 / spread(c0, k)
            ratio = spread(c0, k + 1) * inv0
            inv1 = 1.0 / (spread(c1, k + 1) - ratio * spread(c1, k))
            r0 = jnp.where(lane8 == k, 1.0, jnp.where(lane8 == k + 1, 0.0, spread(a, k)))
            r1 = jnp.where(lane8 == k + 1, 1.0, jnp.where(lane8 == k, 0.0, spread(a, k + 1)))
            y1 = (r1 - ratio * r0) * inv1
            y0 = r0 * inv0 - ratio * y1
            y0 = jnp.broadcast_to(y0[:1], (n, n))
            y1 = jnp.broadcast_to(y1[:1], (n, n))
            new = jnp.where((lane >> 1) == (k >> 1), 0.0, a) - c0 * y0 - c1 * y1
            done.append(jnp.where(row == k, y0, jnp.where(row == k + 1, y1, new)))
        blocks = done
    return blocks


def solve_all(systems, sides):
    n = E
    for p in range(0, n, NB):
        inverses = invert_blocks([s[p : p + NB, p : p + NB] for s in systems])
        next_systems, next_sides = [], []
        for s, r, inverse in zip(systems, sides, inverses):
            last = p + NB == n
            full = r if last else jnp.concatenate([s[:, p + NB :], r], axis=1)
            pivot = exact(inverse, full[p : p + NB])
            parts = []
            if p:
                parts.append(full[:p] - exact(s[:p, p : p + NB], pivot))
            parts.append(pivot)
            if not last:
                parts.append(full[p + NB :] - exact(s[p + NB :, p : p + NB], pivot))
            full = jnp.concatenate(parts, axis=0)
            if not last:
                rest = n - p - NB
                next_systems.append(jnp.concatenate([jnp.zeros((n, p + NB), F32), full[:, :rest]], axis=1))
                full = full[:, rest:]
            next_sides.append(full)
        systems, sides = next_systems, next_sides
    return sides


def merged(outer_left, outer_right, side, solved):
    across = jnp.transpose(side)
    ww = outer_left - exact(across[:E], solved[:, :E])
    low = exact(across[E:], solved)
    return ww, -low[:, :E], outer_right - low[:, E:]


def kernel(
    size_x, size_y,
    mask, traces, leaf, box_maps, box_loads,
    lm, tv, m0, m1, rx, to, te, tc, tx, xt0, q_hi, q_lo, ps, pr, total, a2, xt1, m2, fin,
    local_sem, early_send, early_recv, m0_send, m0_recv, m1_send, m1_recv,
    pr_send, pr_recv, a2_send, a2_recv, fin_send, fin_recv,
):
    gx = lax.axis_index("gx")
    gy = lax.axis_index("gy")
    x = lax.rem(gx, 2)
    y = lax.rem(lax.div(gx, 2), 4)
    base = gx - lax.rem(gx, 8)
    core = lax.rem(gy, 2)
    partner = (gx + 1 - 2 * x, gy)
    back = lax.rem(gx + size_x - 2, size_x)
    ahead = lax.rem(gx + 2, size_x)
    on_chip = (gx, gy + 1 - 2 * core)
    off_chip = (gx + 1 - 2 * x, lax.rem(gy + size_y + 2 * core - 1, size_y))
    outward = (back + x * (ahead - back), gy)
    inward = (ahead + x * (back - ahead), gy)

    def member(step_y, flip):
        other_y = lax.rem(y + step_y, 4)
        other_x = 1 - x if flip else x
        return other_y, other_x, (base + 2 * other_y + other_x, gy)

    members = [member(s, f) for f in (False, True) for s in range(4) if f or s]

    def remote(src, dst, send, recv, to_device):
        return pltpu.make_async_remote_copy(
            src_ref=src, dst_ref=dst, send_sem=send, recv_sem=recv, device_id=to_device, device_id_type=MESH
        )

    barrier = pltpu.get_barrier_semaphore()
    greeted = [m[2] for m in members] + [outward, inward, on_chip, off_chip]
    for device in greeted:
        pl.semaphore_signal(barrier, inc=1, device_id=device, device_id_type=MESH)

    load_maps = pltpu.make_async_copy(leaf.at[0, :, pl.ds(0, 2 * E), :], lm, local_sem.at[0])
    load_maps.start()
    load_traces = pltpu.make_async_copy(traces.at[0], tv, local_sem.at[1])
    load_traces.start()
    mine = pl.ds(pl.multiple_of(x * 512, 512), 512)
    theirs = pl.ds(pl.multiple_of((1 - x) * 512, 512), 512)
    load_outer = pltpu.make_async_copy(traces.at[0, :, x, :, mine], to.at[x], local_sem.at[2])
    load_outer.start()

    load_maps.wait()
    eye = lax.broadcasted_iota(jnp.int32, (E, E), 0) == lax.broadcasted_iota(jnp.int32, (E, E), 1)
    lane_block = lax.div(lax.broadcasted_iota(jnp.int32, (1, E), 1), PB)
    face = pl.ds(pl.multiple_of((1 - x) * E, E), E)
    outer = pl.ds(pl.multiple_of(x * E, E), E)
    for j in range(2):
        for kind, edge, span in ((0, 1 - x, face), (2, x, outer)):
            ports = jnp.zeros((1, E), F32)
            for b in range(E // PB):
                ports = jnp.where(lane_block == b, decap_admittance * mask[0, j, edge, b].astype(F32), ports)
            m0[x, kind, j] = lm[j, span, span] + jnp.where(eye, ports, 0.0)
        m0[x, 1, j] = lm[j, face, outer]

    pl.semaphore_wait(barrier, len(greeted))
    sends = []

    def begin(copy):
        copy.start()
        sends.append(copy)
        return copy

    row_out = 1 - core
    row_off = core
    m0_copies = [begin(remote(m0.at[x, k], m0.at[x, k], m0_send.at[k], m0_recv.at[k], partner)) for k in range(3)]
    copy_tc = begin(remote(traces.at[0, row_out, 3 - core], tc, early_send.at[0], early_recv.at[0], on_chip))
    copy_tx = begin(remote(traces.at[0, row_off, 2 + core], tx, early_send.at[1], early_recv.at[1], off_chip))
    copy_out = begin(remote(traces.at[0, :, x, :, mine], te.at[1 - x], early_send.at[2], early_recv.at[2], outward))
    edge_off = pl.ds(pl.multiple_of((2 + core) * E, E), E)
    copy_rx = begin(
        remote(leaf.at[0, row_off, pl.ds(0, 2 * E), edge_off], rx, early_send.at[3], early_recv.at[3], partner)
    )

    def m0_other(k):
        return remote(m0.at[1 - x, k], m0.at[1 - x, k], m0_send.at[k], m0_recv.at[k], partner)

    for k in range(3):
        m0_other(k).wait_recv()
    copy_to = begin(remote(traces.at[0, :, x, :, theirs], to.at[x], early_send.at[4], early_recv.at[4], partner))

    systems = [m0[0, 0, j] + m0[1, 0, j] for j in range(2)]
    sides = [jnp.concatenate([m0[0, 1, j], m0[1, 1, j]], axis=1) for j in range(2)]
    solved = solve_all(systems, sides)
    for j in range(2):
        ww, ew, ee = merged(m0[0, 2, j], m0[1, 2, j], sides[j], solved[j])
        m1[y, j, 0] = ww
        m1[y, j, 1] = ew
        m1[y, j, 2] = ee
        xt0[j] = jnp.transpose(solved[j])
    for s in range(1, 4):
        begin(remote(m1.at[y], m1.at[y], m1_send.at[s], m1_recv.at[y], member(s, False)[2]))

    remote(to.at[1 - x], to.at[1 - x], early_send.at[4], early_recv.at[4], partner).wait_recv()
    begin(remote(to.at[1 - x], te.at[x], early_send.at[5], early_recv.at[5], inward))

    load_traces.wait()
    copy_rx.wait_recv()
    xf = x.astype(F32)

    def placed(block, right):
        return jnp.concatenate([block * (1.0 - right), block * right], axis=0)

    for row, off in ((row_out, False), (row_off, True)):
        inner = pl.ds(pl.multiple_of((3 - row) * E, E), E)
        rim = pl.ds(pl.multiple_of((2 + row) * E, E), E)
        xt = xt0[row]
        through = [m0[0, 0, row] + m0[1, 0, row], lm[row, face, inner], lm[row, face, rim]]
        direct = [
            jnp.transpose(jnp.concatenate([m0[0, 1, row], m0[1, 1, row]], axis=1)),
            placed(lm[row, outer, inner], xf),
            placed(lm[row, outer, rim], xf),
        ]
        if off:
            through.append(rx[outer, :])
            direct.append(placed(rx[face, :], 1.0 - xf))
        coefficient = 0.5 * (jnp.concatenate(direct, axis=1) - exact(xt, jnp.concatenate(through, axis=1)))
        high, low = halves(coefficient)
        width = coefficient.shape[1]
        q_hi[row, :, :width] = high
        q_lo[row, :, :width] = low

    copy_tc.wait_recv()
    copy_tx.wait_recv()

    def partial_load(start, slot):
        columns = pl.ds(pl.multiple_of(start, 256), 256)
        seam = tv[0, 3, :, columns] + tv[1, 2, :, columns]
        for row, off in ((row_out, False), (row_off, True)):
            rim = tv[row, 2 + row, :, columns]
            parts = [tv[row, 1 - x, :, columns], seam]
            parts += [rim, tx[:, columns]] if off else [rim + tc[:, columns]]
            data = jnp.concatenate(parts, axis=0)
            width = data.shape[0]
            load = split_dot((q_hi[row, :, :width], q_lo[row, :, :width]), halves(data))
            ps[slot, row] = load[:, :E]
            ps[slot + 1, row] = load[:, E:]

    for i in range(2):
        partial_load((1 - x) * 512 + i * 256, (1 - x) * 4 + 2 * i)
        for q in (2 * i, 2 * i + 1):
            begin(remote(ps.at[(1 - x) * 4 + q], pr.at[q], pr_send.at[q], pr_recv.at[q], partner))
    for i in range(2):
        partial_load(x * 512 + i * 256, x * 4 + 2 * i)

    for s in range(1, 4):
        other = member(s, False)
        remote(m1.at[y], m1.at[other[0]], m1_send.at[s], m1_recv.at[other[0]], other[2]).wait_recv()
    pairs = [(m, j) for m in range(2) for j in range(2)]
    systems = [m1[2 * m, j, 2] + m1[2 * m + 1, j, 0] for m, j in pairs]
    sides = [jnp.concatenate([m1[2 * m, j, 1], jnp.transpose(m1[2 * m + 1, j, 1])], axis=1) for m, j in pairs]
    solved = solve_all(systems, sides)
    for (m, j), side, s in zip(pairs, sides, solved):
        ww, ew, ee = merged(m1[2 * m, j, 0], m1[2 * m + 1, j, 2], side, s)
        m2[m, j, 0] = ww
        m2[m, j, 1] = ew
        m2[m, j, 2] = ee
        xt1[m, j] = jnp.transpose(s)

    load_outer.wait()
    remote(to.at[1 - x], te.at[1 - x], early_send.at[2], early_recv.at[2], inward).wait_recv()
    remote(to.at[1 - x], te.at[x], early_send.at[5], early_recv.at[5], outward).wait_recv()
    alphas = []
    for j in range(2):
        top = jnp.concatenate([m1[y, j, 0], jnp.transpose(m1[y, j, 1])], axis=1)
        bottom = jnp.concatenate([m1[y, j, 1], m1[y, j, 2]], axis=1)
        alphas.append(halves(0.5 * jnp.concatenate([top, bottom], axis=0)))
    for s in (1, 2, 3, 0):
        q, _, device = member(s, False)
        remote(ps.at[q], pr.at[q], pr_send.at[q], pr_recv.at[q], partner).wait_recv()
        columns = pl.ds(pl.multiple_of(q * E, E), E)
        for j in range(2):
            data = jnp.concatenate([to[e, j, :, columns] + te[e, j, :, columns] for e in range(2)], axis=0)
            load = ps[x * 4 + q, j] + pr[q, j] + split_dot(alphas[j], halves(data))
            if s:
                total[q, j] = load
            else:
                a2[y, j] = load
        if s:
            begin(remote(total.at[q], a2.at[y], a2_send.at[s], a2_recv.at[y], device))

    systems = [m2[0, j, 2] + m2[1, j, 0] for j in range(2)]
    sides = [jnp.concatenate([m2[0, j, 1], jnp.transpose(m2[1, j, 1])], axis=1) for j in range(2)]
    solved = solve_all(systems, sides)
    last = [jnp.transpose(s) for s in solved]

    for s in range(1, 4):
        other = member(s, False)
        remote(total.at[0], a2.at[other[0]], a2_send.at[s], a2_recv.at[other[0]], other[2]).wait_recv()
    for j in range(2):
        boxes = []
        for m in range(2):
            left, right = a2[2 * m, j], a2[2 * m + 1, j]
            ends = jnp.concatenate([left[:E], right[E:]], axis=0)
            boxes.append(ends - near(xt1[m, j], left[E:] + right[:E]))
        left, right = boxes
        ends = jnp.concatenate([left[:E], right[E:]], axis=0)
        fin[j] = ends - near(last[j], left[E:] + right[:E])
    own = pl.ds(pl.multiple_of((x * 4 + y) * E, E), E)
    for i, (_, _, device) in enumerate(members):
        begin(remote(fin, box_loads.at[0, :, :, own], fin_send.at[i], fin_recv.at[x * 4 + y], device))
    keep = pltpu.make_async_copy(fin, box_loads.at[0, :, :, own], local_sem.at[3])
    keep.start()

    for j in range(2):
        ww, ew, ee = merged(m2[0, j, 0], m2[1, j, 2], sides[j], solved[j])
        box_maps[0, j, :E, :E] = ww
        box_maps[0, j, E:, :E] = ew
        box_maps[0, j, :E, E:] = jnp.transpose(ew)
        box_maps[0, j, E:, E:] = ee

    for other_y, other_x, device in members:
        slot = other_x * 4 + other_y
        columns = pl.ds(pl.multiple_of(slot * E, E), E)
        remote(fin, box_loads.at[0, :, :, columns], fin_send.at[0], fin_recv.at[slot], device).wait_recv()
    keep.wait()
    for copy in sends:
        copy.wait_send()


def body(traces, leaf_maps, decap_mask):
    size_x, size_y = lax.axis_size("gx"), lax.axis_size("gy")
    dma = pltpu.SemaphoreType.DMA
    return pl.pallas_call(
        functools.partial(kernel, size_x, size_y),
        out_shape=(
            jax.ShapeDtypeStruct((1, 2, 2 * E, 2 * E), F32),
            jax.ShapeDtypeStruct((1, 2, 2 * E, K), F32),
        ),
        in_specs=[
            pl.BlockSpec(memory_space=pltpu.SMEM),
            pl.BlockSpec(memory_space=pl.ANY),
            pl.BlockSpec(memory_space=pl.ANY),
        ],
        out_specs=(pl.BlockSpec(memory_space=pltpu.VMEM), pl.BlockSpec(memory_space=pl.ANY)),
        scratch_shapes=[
            pltpu.VMEM((2, 2 * E, 4 * E), F32),
            pltpu.VMEM((2, 4, E, K), F32),
            pltpu.VMEM((2, 3, 2, E, E), F32),
            pltpu.VMEM((4, 2, 3, E, E), F32),
            pltpu.VMEM((2 * E, E), F32),
            pltpu.VMEM((2, 2, E, 512), F32),
            pltpu.VMEM((2, 2, E, 512), F32),
            pltpu.VMEM((E, K), F32),
            pltpu.VMEM((E, K), F32),
            pltpu.VMEM((2, 2 * E, E), F32),
            pltpu.VMEM((2, 2 * E, 4 * E), BF16),
            pltpu.VMEM((2, 2 * E, 4 * E), BF16),
            pltpu.VMEM((8, 2, 2 * E, E), F32),
            pltpu.VMEM((4, 2, 2 * E, E), F32),
            pltpu.VMEM((4, 2, 2 * E, E), F32),
            pltpu.VMEM((4, 2, 2 * E, E), F32),
            pltpu.VMEM((2, 2, 2 * E, E), F32),
            pltpu.VMEM((2, 2, 3, E, E), F32),
            pltpu.VMEM((2, 2 * E, E), F32),
            dma((4,)), dma((6,)), dma((6,)), dma((3,)), dma((3,)), dma((4,)), dma((4,)),
            dma((4,)), dma((4,)), dma((4,)), dma((4,)), dma((7,)), dma((8,)),
        ],
        compiler_params=pltpu.CompilerParams(
            collective_id=0, has_side_effects=True, vmem_limit_bytes=48 * 1024 * 1024
        ),
    )(decap_mask, traces, leaf_maps)


def solution(mesh):
    placed = (P("gx", "gy", None, None, None), P("gx", "gy", None, None), P("gx", "gy", None, None))
    return jax.shard_map(
        body,
        mesh=mesh,
        in_specs=placed,
        out_specs=(P("gx", "gy", None, None), P("gx", "gy", None, None)),
        check_vma=False,
    )
```

time: 446 us -> 128 us (0.29); the launches traced: 437 us -> 128 us
  waiting for transfers between devices: 218 us -> 0 us
  other arithmetic: 167 us -> 0 us
  Pallas kernels: 0 us -> 123 us
  matrix products: 23.5 us -> 0 us
  starting transfers between devices: 15.9 us -> 0 us
  local copies, waits for them, and re-layouts: 11.9 us -> 4.38 us
    ppermute x10 -> x0, waiting for transfers between devices: 218 us -> none  [the longest x6 169 us: from_partner(): return lax.ppermute(block, axis, route)]
    another operation x19 -> x0, other arithmetic: 145 us -> none  [the longest x10 82.8 us: solve_inter(): factor = jnp.linalg.cholesky(inter)]
    pallas_call x0 -> x1, Pallas kernels: none -> 123 us  [body(): pl.pallas_call(functools.partial(kernel, size_x, size_y), out_shape=(jax....]
    dot_general x19 -> x0, matrix products: 16.1 us -> none  [matprod(): return jnp.matmul(left, right, precision=lax.Precision.HIGHEST)]
    ppermute x10 -> x0, starting transfers between devices: 15.9 us -> none  [the longest x6 11.9 us: from_partner(): return lax.ppermute(block, axis, route)]
    select_n x6 -> x0, other arithmetic: 10.5 us -> none  [the longest x3 7.1 us: body(): left_load = jnp.where(is_left, box_load, other_load)]
    another operation x6 -> x0, matrix products: 7.48 us -> none  [the longest x3 3.84 us: solve_inter(): half = jax.scipy.linalg.solve_triangular(factor, stacked, lower=True)]
    squeeze x2 -> x0, local copies, waits for them, and re-layouts: 4.68 us -> none  [the longest x1 3.29 us: body(): from_west = passed_along(traces[:, :, 1], 'gx', 1)]
  transfers between devices with their start and end apart: 10 -> 0, of which waited for: 5 -> 0; matrix products, arithmetic and copies ran while one was open for 36% -> 0% of each run, Pallas kernels for 0% -> 0%
where the time goes in v1:
time: 128 us
  Pallas kernels  123 us (96%)
  local copies, waits for them, and re-layouts  4.38 us (3%)
    pallas_call x1, Pallas kernels, body(): pl.pallas_call(functools.partial(kernel, size_x, size_y), out_shape=(jax....  123 us
    unnamed x6, local copies, waits for them, and re-layouts  4.38 us

profile of v1, /device:TPU:8, one launch (start us, length us, event | category | flops | bytes accessed | tf_op | source)
XLA Modules:
  0.0 127.8 jit_solution(13865971171511954035)
XLA Ops:
  0.6 0.0 copy-start
  0.6 1.6 %copy-done = f32[1,2,512,512]{3,2,1,0:T(8,128)S(1)} copy-done((f32[1,2,512,512]{3,2,1,0:T(8,128)S(1)}, f32[1,2,512,512]{3,2,1,0:T(8,128)}, u32[]{:S(2)}) %copy-start) | copy-done | bytes 2097176
  2.2 0.0 copy-start.1
  2.2 0.7 copy-done.1
  2.9 122.7 %shard_map.50 = (f32[1,2,256,256]{3,2,1,0:T(8,128)S(1)}, f32[1,2,256,1024]{3,2,1,0:T(8,128)S(1)}) custom-call(s32[1,2,4,8]{3,2,1,0:T(4,128)S(1)} %copy-done.1, f32[1,2,4,128,1024]{4,3,2,1,0:T(8,128)} %traces.1, f32[1,2,512,512]{3,2,1,0:T(8,128)S(1)} %copy-done), custom_call_target="tpu_custom_call" | custom-call | tf_op jit(solution)/shard_map/pallas_call | solution.py:330
  125.6 0.8 copy.7
  126.4 1.3 %copy.8 = f32[1,2,256,1024]{3,2,1,0:T(8,128)} copy(f32[1,2,256,1024]{3,2,1,0:T(8,128)S(1)} %get-tuple-element.5) | data formatting | bytes 4194304
Async XLA Ops:
  0.6 1.6 %copy-start = (f32[1,2,512,512]{3,2,1,0:T(8,128)S(1)}, f32[1,2,512,512]{3,2,1,0:T(8,128)}, u32[]{:S(2)}) copy-start(f32[1,2,512,512]{3,2,1,0:T(8,128)} %leaf.1) | copy-start | bytes 6291460
  2.2 0.7 copy-start.1

commit v2 on v1

--- a/solution.py
+++ b/solution.py
@@ -13,6 +13,7 @@
 F32 = jnp.float32
 BF16 = jnp.bfloat16
 NB = 32
+STEP = 4
 MESH = pl.DeviceIdType.MESH
 
 decap_admittance = 2.0
@@ -38,42 +39,58 @@
     return split_dot(halves(left), halves(right))
 
 
-def invert_blocks(blocks):
-    n = blocks[0].shape[0]
-    lane = lax.broadcasted_iota(jnp.int32, (n, n), 1)
-    row = lax.broadcasted_iota(jnp.int32, (n, n), 0)
-    lane8 = lane[:8]
-    for k in range(0, n, 2):
-        done = []
-        for a in blocks:
-            c0 = jnp.broadcast_to(a[:, k : k + 1], (n, n))
-            c1 = jnp.broadcast_to(a[:, k + 1 : k + 2], (n, n))
-
-            def spread(v, i):
-                return jnp.broadcast_to(v[i : i + 1, :], (8, n))
-
-            inv0 = 1.0 / spread(c0, k)
-            ratio = spread(c0, k + 1) * inv0
-            inv1 = 1.0 / (spread(c1, k + 1) - ratio * spread(c1, k))
-            r0 = jnp.where(lane8 == k, 1.0, jnp.where(lane8 == k + 1, 0.0, spread(a, k)))
-            r1 = jnp.where(lane8 == k + 1, 1.0, jnp.where(lane8 == k, 0.0, spread(a, k + 1)))
-            y1 = (r1 - ratio * r0) * inv1
-            y0 = r0 * inv0 - ratio * y1
-            y0 = jnp.broadcast_to(y0[:1], (n, n))
-            y1 = jnp.broadcast_to(y1[:1], (n, n))
-            new = jnp.where((lane >> 1) == (k >> 1), 0.0, a) - c0 * y0 - c1 * y1
-            done.append(jnp.where(row == k, y0, jnp.where(row == k + 1, y1, new)))
-        blocks = done
-    return blocks
+def invert_blocks(packed):
+    shape = packed.shape
+    lane = lax.broadcasted_iota(jnp.int32, shape, 1)
+    row = lax.broadcasted_iota(jnp.int32, shape, 0)
+    place = lax.rem(lane, NB)
+    block = lane - place
+    place8, block8 = place[:8], block[:8]
+    steps = range(STEP)
+    for k in range(0, NB, STEP):
+        columns = [jnp.take_along_axis(packed, block + (k + j), axis=1) for j in steps]
+        rows = [jnp.broadcast_to(packed[k + i : k + i + 1, :], (8, shape[1])) for i in steps]
+        a = [[jnp.take_along_axis(rows[i], block8 + (k + j), axis=1) for j in steps] for i in steps]
+        pivots8 = (place8 >= k) & (place8 < k + STEP)
+        rows = [jnp.where(place8 == k + i, 1.0, jnp.where(pivots8, 0.0, rows[i])) for i in steps]
+        for p in steps:
+            inverse = 1.0 / a[p][p]
+            factors = [a[i][p] for i in steps]
+            for j in range(p + 1, STEP):
+                a[p][j] = a[p][j] * inverse
+            rows[p] = rows[p] * inverse
+            for i in steps:
+                if i != p:
+                    for j in range(p + 1, STEP):
+                        a[i][j] = a[i][j] - factors[i] * a[p][j]
+                    rows[i] = rows[i] - factors[i] * rows[p]
+        wide = [jnp.broadcast_to(r[:1], shape) for r in rows]
+        new = jnp.where((place >= k) & (place < k + STEP), 0.0, packed)
+        for j in steps:
+            new = new - columns[j] * wide[j]
+        for j in steps:
+            new = jnp.where(row == k + j, wide[j], new)
+        packed = new
+    return packed
 
 
 def solve_all(systems, sides):
     n = E
+    blocks = [s[:NB, :NB] for s in systems]
     for p in range(0, n, NB):
-        inverses = invert_blocks([s[p : p + NB, p : p + NB] for s in systems])
+        packed = invert_blocks(jnp.concatenate([blocks[i % len(blocks)] for i in range(E // NB)], axis=1))
+        inverses = [packed[:, i * NB : (i + 1) * NB] for i in range(len(blocks))]
+        if callable(sides):
+            sides = sides()
+        last = p + NB == n
+        if not last:
+            ahead = slice(p + NB, p + 2 * NB)
+            blocks = [
+                s[ahead, ahead] - exact(s[ahead, p : p + NB], exact(inverse, s[p : p + NB, ahead]))
+                for s, inverse in zip(systems, inverses)
+            ]
         next_systems, next_sides = [], []
         for s, r, inverse in zip(systems, sides, inverses):
-            last = p + NB == n
             full = r if last else jnp.concatenate([s[:, p + NB :], r], axis=1)
             pivot = exact(inverse, full[p : p + NB])
             parts = []
@@ -102,9 +119,9 @@
 def kernel(
     size_x, size_y,
     mask, traces, leaf, box_maps, box_loads,
-    lm, tv, m0, m1, rx, to, te, tc, tx, xt0, q_hi, q_lo, ps, pr, total, a2, xt1, m2, fin,
+    lm, tv, m0, m1, rx, to, te, tc, tx, xt0, ends, q_hi, q_lo, ps, pr, total, a2, xt1, m2, fin, got,
     local_sem, early_send, early_recv, m0_send, m0_recv, m1_send, m1_recv,
-    pr_send, pr_recv, a2_send, a2_recv, fin_send, fin_recv,
+    pr_send, pr_recv, a2_send, a2_recv, fin_send, fin_recv, keep_sem,
 ):
     gx = lax.axis_index("gx")
     gy = lax.axis_index("gy")
@@ -141,10 +158,6 @@
     load_maps.start()
     load_traces = pltpu.make_async_copy(traces.at[0], tv, local_sem.at[1])
     load_traces.start()
-    mine = pl.ds(pl.multiple_of(x * 512, 512), 512)
-    theirs = pl.ds(pl.multiple_of((1 - x) * 512, 512), 512)
-    load_outer = pltpu.make_async_copy(traces.at[0, :, x, :, mine], to.at[x], local_sem.at[2])
-    load_outer.start()
 
     load_maps.wait()
     eye = lax.broadcasted_iota(jnp.int32, (E, E), 0) == lax.broadcasted_iota(jnp.int32, (E, E), 1)
@@ -172,30 +185,50 @@
     m0_copies = [begin(remote(m0.at[x, k], m0.at[x, k], m0_send.at[k], m0_recv.at[k], partner)) for k in range(3)]
     copy_tc = begin(remote(traces.at[0, row_out, 3 - core], tc, early_send.at[0], early_recv.at[0], on_chip))
     copy_tx = begin(remote(traces.at[0, row_off, 2 + core], tx, early_send.at[1], early_recv.at[1], off_chip))
-    copy_out = begin(remote(traces.at[0, :, x, :, mine], te.at[1 - x], early_send.at[2], early_recv.at[2], outward))
+    mine = pl.ds(pl.multiple_of(x * 512, 512), 512)
+    theirs = pl.ds(pl.multiple_of((1 - x) * 512, 512), 512)
+    load_outer = pltpu.make_async_copy(traces.at[0, :, x, :, mine], to.at[x], local_sem.at[2])
+    load_outer.start()
+    begin(remote(traces.at[0, :, x, :, mine], te.at[1 - x], early_send.at[3], early_recv.at[3], outward))
     edge_off = pl.ds(pl.multiple_of((2 + core) * E, E), E)
-    copy_rx = begin(
-        remote(leaf.at[0, row_off, pl.ds(0, 2 * E), edge_off], rx, early_send.at[3], early_recv.at[3], partner)
-    )
 
     def m0_other(k):
         return remote(m0.at[1 - x, k], m0.at[1 - x, k], m0_send.at[k], m0_recv.at[k], partner)
 
-    for k in range(3):
-        m0_other(k).wait_recv()
-    copy_to = begin(remote(traces.at[0, :, x, :, theirs], to.at[x], early_send.at[4], early_recv.at[4], partner))
+    m0_other(0).wait_recv()
+    copy_rx = begin(
+        remote(leaf.at[0, row_off, pl.ds(0, 2 * E), edge_off], rx, early_send.at[2], early_recv.at[2], partner)
+    )
 
     systems = [m0[0, 0, j] + m0[1, 0, j] for j in range(2)]
+
+    def pair_sides():
+        m0_other(1).wait_recv()
+        begin(remote(traces.at[0, :, x, :, theirs], to.at[x], early_send.at[4], early_recv.at[4], partner))
+        return [jnp.concatenate([m0[0, 1, j], m0[1, 1, j]], axis=1) for j in range(2)]
+
+    solved = solve_all(systems, pair_sides)
     sides = [jnp.concatenate([m0[0, 1, j], m0[1, 1, j]], axis=1) for j in range(2)]
-    solved = solve_all(systems, sides)
+    m0_other(2).wait_recv()
     for j in range(2):
         ww, ew, ee = merged(m0[0, 2, j], m0[1, 2, j], sides[j], solved[j])
-        m1[y, j, 0] = ww
-        m1[y, j, 1] = ew
-        m1[y, j, 2] = ee
+        m1[y, 0, j] = ww
+        m1[y, 1, j] = ew
+        m1[y, 2, j] = ee
         xt0[j] = jnp.transpose(solved[j])
-    for s in range(1, 4):
-        begin(remote(m1.at[y], m1.at[y], m1_send.at[s], m1_recv.at[y], member(s, False)[2]))
+        ends[j, :E] = 0.5 * jnp.concatenate([ww, jnp.transpose(ew)], axis=1)
+        ends[j, E:] = 0.5 * jnp.concatenate([ew, ee], axis=1)
+
+    def m1_copy(s, order, owner, device):
+        first = 2 * (1 - lax.rem(owner, 2))
+        kind = (first, 1, 2 - first)[order]
+        return remote(
+            m1.at[owner, kind], m1.at[owner, kind], m1_send.at[order, s], m1_recv.at[order, owner], device
+        )
+
+    for order in range(3):
+        for s in (1, 3, 2):
+            begin(m1_copy(s, order, y, member(s, False)[2]))
 
     remote(to.at[1 - x], to.at[1 - x], early_send.at[4], early_recv.at[4], partner).wait_recv()
     begin(remote(to.at[1 - x], te.at[x], early_send.at[5], early_recv.at[5], inward))
@@ -229,8 +262,10 @@
     copy_tc.wait_recv()
     copy_tx.wait_recv()
 
-    def partial_load(start, slot):
-        columns = pl.ds(pl.multiple_of(start, 256), 256)
+    def partial_load(i):
+        half = lax.rem(1 - x + i // 2, 2)
+        slot = half * 4 + 2 * (i % 2)
+        columns = pl.ds(pl.multiple_of(half * 512 + (i % 2) * 256, 256), 256)
         seam = tv[0, 3, :, columns] + tv[1, 2, :, columns]
         for row, off in ((row_out, False), (row_off, True)):
             rim = tv[row, 2 + row, :, columns]
@@ -243,47 +278,56 @@
             ps[slot + 1, row] = load[:, E:]
 
     for i in range(2):
-        partial_load((1 - x) * 512 + i * 256, (1 - x) * 4 + 2 * i)
+        partial_load(i)
         for q in (2 * i, 2 * i + 1):
             begin(remote(ps.at[(1 - x) * 4 + q], pr.at[q], pr_send.at[q], pr_recv.at[q], partner))
     for i in range(2):
-        partial_load(x * 512 + i * 256, x * 4 + 2 * i)
+        partial_load(2 + i)
 
     for s in range(1, 4):
         other = member(s, False)
-        remote(m1.at[y], m1.at[other[0]], m1_send.at[s], m1_recv.at[other[0]], other[2]).wait_recv()
+        for order in range(2):
+            m1_copy(s, order, other[0], other[2]).wait_recv()
     pairs = [(m, j) for m in range(2) for j in range(2)]
-    systems = [m1[2 * m, j, 2] + m1[2 * m + 1, j, 0] for m, j in pairs]
-    sides = [jnp.concatenate([m1[2 * m, j, 1], jnp.transpose(m1[2 * m + 1, j, 1])], axis=1) for m, j in pairs]
+    systems = [m1[2 * m, 2, j] + m1[2 * m + 1, 0, j] for m, j in pairs]
+    sides = [jnp.concatenate([m1[2 * m, 1, j], jnp.transpose(m1[2 * m + 1, 1, j])], axis=1) for m, j in pairs]
     solved = solve_all(systems, sides)
+    for s in range(1, 4):
+        other = member(s, False)
+        m1_copy(s, 2, other[0], other[2]).wait_recv()
     for (m, j), side, s in zip(pairs, sides, solved):
-        ww, ew, ee = merged(m1[2 * m, j, 0], m1[2 * m + 1, j, 2], side, s)
+        ww, ew, ee = merged(m1[2 * m, 0, j], m1[2 * m + 1, 2, j], side, s)
         m2[m, j, 0] = ww
         m2[m, j, 1] = ew
         m2[m, j, 2] = ee
         xt1[m, j] = jnp.transpose(s)
 
     load_outer.wait()
-    remote(to.at[1 - x], te.at[1 - x], early_send.at[2], early_recv.at[2], inward).wait_recv()
+    remote(to.at[1 - x], te.at[1 - x], early_send.at[3], early_recv.at[3], inward).wait_recv()
     remote(to.at[1 - x], te.at[x], early_send.at[5], early_recv.at[5], outward).wait_recv()
-    alphas = []
-    for j in range(2):
-        top = jnp.concatenate([m1[y, j, 0], jnp.transpose(m1[y, j, 1])], axis=1)
-        bottom = jnp.concatenate([m1[y, j, 1], m1[y, j, 2]], axis=1)
-        alphas.append(halves(0.5 * jnp.concatenate([top, bottom], axis=0)))
-    for s in (1, 2, 3, 0):
-        q, _, device = member(s, False)
+    alphas = [halves(ends[j]) for j in range(2)]
+
+    def share(q):
+        device = (base + 2 * q + x, gy)
+        return remote(total.at[q], a2.at[y], a2_send.at[q], a2_recv.at[y], device)
+
+    def pair_load(q):
         remote(ps.at[q], pr.at[q], pr_send.at[q], pr_recv.at[q], partner).wait_recv()
-        columns = pl.ds(pl.multiple_of(q * E, E), E)
         for j in range(2):
+            columns = slice(q * E, (q + 1) * E)
             data = jnp.concatenate([to[e, j, :, columns] + te[e, j, :, columns] for e in range(2)], axis=0)
-            load = ps[x * 4 + q, j] + pr[q, j] + split_dot(alphas[j], halves(data))
-            if s:
-                total[q, j] = load
-            else:
-                a2[y, j] = load
-        if s:
-            begin(remote(total.at[q], a2.at[y], a2_send.at[s], a2_recv.at[y], device))
+            total[q, j] = ps[x * 4 + q, j] + pr[q, j] + split_dot(alphas[j], halves(data))
+
+        @pl.when(y != q)
+        def _():
+            share(q).start()
+
+        @pl.when(y == q)
+        def _():
+            a2[q] = total[q]
+
+    for q in range(4):
+        pair_load(q)
 
     systems = [m2[0, j, 2] + m2[1, j, 0] for j in range(2)]
     sides = [jnp.concatenate([m2[0, j, 1], jnp.transpose(m2[1, j, 1])], axis=1) for j in range(2)]
@@ -293,20 +337,51 @@
     for s in range(1, 4):
         other = member(s, False)
         remote(total.at[0], a2.at[other[0]], a2_send.at[s], a2_recv.at[other[0]], other[2]).wait_recv()
-    for j in range(2):
+    own_slot = x * 4 + y
+    others = [member(s, False) for s in (1, 3, 2)]
+
+    def gather(n, src, row, slot, device):
+        dst = got.at[row, slot]
+        return remote(dst if src is None else src, dst, fin_send.at[n], fin_recv.at[row, slot], device)
+
+    keeps = []
+
+    def keep(src, row, slot):
+        columns = pl.ds(pl.multiple_of(slot * E, E), E)
+        copy = pltpu.make_async_copy(src, box_loads.at[0, row, :, columns], keep_sem.at[row, slot])
+        copy.start()
+        keeps.append(copy)
+
+    def arrive(n, row, slot, device):
+        gather(n, fin.at[row], row, slot, device).wait_recv()
+        keep(got.at[row, slot], row, slot)
+
+    for j in (0, 1):
         boxes = []
         for m in range(2):
             left, right = a2[2 * m, j], a2[2 * m + 1, j]
-            ends = jnp.concatenate([left[:E], right[E:]], axis=0)
-            boxes.append(ends - near(xt1[m, j], left[E:] + right[:E]))
+            kept = jnp.concatenate([left[:E], right[E:]], axis=0)
+            boxes.append(kept - near(xt1[m, j], left[E:] + right[:E]))
         left, right = boxes
-        ends = jnp.concatenate([left[:E], right[E:]], axis=0)
-        fin[j] = ends - near(last[j], left[E:] + right[:E])
-    own = pl.ds(pl.multiple_of((x * 4 + y) * E, E), E)
-    for i, (_, _, device) in enumerate(members):
-        begin(remote(fin, box_loads.at[0, :, :, own], fin_send.at[i], fin_recv.at[x * 4 + y], device))
-    keep = pltpu.make_async_copy(fin, box_loads.at[0, :, :, own], local_sem.at[3])
-    keep.start()
+        kept = jnp.concatenate([left[:E], right[E:]], axis=0)
+        fin[j] = kept - near(last[j], left[E:] + right[:E])
+        begin(gather(7 * j, fin.at[j], j, own_slot, partner))
+        for i, (_, _, device) in enumerate(others):
+            begin(gather(7 * j + 1 + i, fin.at[j], j, own_slot, device))
+        keep(fin.at[j], j, own_slot)
+
+    partner_slot = (1 - x) * 4 + y
+    def pass_on(i):
+        slot = x * 4 + others[i][0]
+        arrive(1 + i, 0, slot, others[i][2])
+        begin(gather(4 + i, None, 0, slot, partner))
+
+    pass_on(0)
+    pass_on(1)
+    arrive(7, 1, partner_slot, partner)
+    for i, (_, _, device) in enumerate(others):
+        begin(gather(11 + i, None, 1, partner_slot, device))
+    pass_on(2)
 
     for j in range(2):
         ww, ew, ee = merged(m2[0, j, 0], m2[1, j, 2], sides[j], solved[j])
@@ -315,13 +390,20 @@
         box_maps[0, j, :E, E:] = jnp.transpose(ew)
         box_maps[0, j, E:, E:] = ee
 
-    for other_y, other_x, device in members:
-        slot = other_x * 4 + other_y
-        columns = pl.ds(pl.multiple_of(slot * E, E), E)
-        remote(fin, box_loads.at[0, :, :, columns], fin_send.at[0], fin_recv.at[slot], device).wait_recv()
-    keep.wait()
+    for i, (other_y, _, device) in enumerate(others):
+        arrive(8 + i, 1, x * 4 + other_y, device)
+        arrive(11 + i, 1, (1 - x) * 4 + other_y, device)
+    arrive(0, 0, partner_slot, partner)
+    for i, (other_y, _, _) in enumerate(others):
+        arrive(4 + i, 0, (1 - x) * 4 + other_y, partner)
+    for copy in keeps:
+        copy.wait()
     for copy in sends:
         copy.wait_send()
+    for q in range(4):
+        @pl.when(y != q)
+        def _(q=q):
+            share(q).wait_send()
 
 
 def body(traces, leaf_maps, decap_mask):
@@ -343,13 +425,14 @@
             pltpu.VMEM((2, 2 * E, 4 * E), F32),
             pltpu.VMEM((2, 4, E, K), F32),
             pltpu.VMEM((2, 3, 2, E, E), F32),
-            pltpu.VMEM((4, 2, 3, E, E), F32),
+            pltpu.VMEM((4, 3, 2, E, E), F32),
             pltpu.VMEM((2 * E, E), F32),
             pltpu.VMEM((2, 2, E, 512), F32),
             pltpu.VMEM((2, 2, E, 512), F32),
             pltpu.VMEM((E, K), F32),
             pltpu.VMEM((E, K), F32),
             pltpu.VMEM((2, 2 * E, E), F32),
+            pltpu.VMEM((2, 2 * E, 2 * E), F32),
             pltpu.VMEM((2, 2 * E, 4 * E), BF16),
             pltpu.VMEM((2, 2 * E, 4 * E), BF16),
             pltpu.VMEM((8, 2, 2 * E, E), F32),
@@ -359,11 +442,12 @@
             pltpu.VMEM((2, 2, 2 * E, E), F32),
             pltpu.VMEM((2, 2, 3, E, E), F32),
             pltpu.VMEM((2, 2 * E, E), F32),
-            dma((4,)), dma((6,)), dma((6,)), dma((3,)), dma((3,)), dma((4,)), dma((4,)),
-            dma((4,)), dma((4,)), dma((4,)), dma((4,)), dma((7,)), dma((8,)),
+            pltpu.VMEM((2, 8, 2 * E, E), F32),
+            dma((3,)), dma((6,)), dma((6,)), dma((3,)), dma((3,)), dma((3, 4)), dma((3, 4)),
+            dma((4,)), dma((4,)), dma((4,)), dma((4,)), dma((14,)), dma((2, 8)), dma((2, 8)),
         ],
         compiler_params=pltpu.CompilerParams(
-            collective_id=0, has_side_effects=True, vmem_limit_bytes=48 * 1024 * 1024
+            collective_id=0, has_side_effects=True, vmem_limit_bytes=60 * 1024 * 1024
         ),
     )(decap_mask, traces, leaf_maps)
 

time: 128 us -> 98.4 us (0.77)
  the two profiles are of different devices: /device:TPU:8 before, /device:TPU:14 now
where the time goes in v2:
time: 98.4 us; the launch traced here: 98.2 us
  Pallas kernels  92.6 us (94%)
  local copies, waits for them, and re-layouts  5.03 us (5%)
    pallas_call x1, Pallas kernels, body(): pl.pallas_call(functools.partial(kernel, size_x, size_y), out_shape=(jax....  92.6 us
    unnamed x2, local copies, waits for them, and re-layouts  5.03 us

profile of v2, /device:TPU:14, one launch (start us, length us, event | category | flops | bytes accessed | tf_op | source)
XLA Modules:
  0.0 98.2 jit_solution(9496434028215917616)
XLA Ops:
  0.6 92.6 %shard_map.50 = (f32[1,2,256,256]{3,2,1,0:T(8,128)}, f32[1,2,256,1024]{3,2,1,0:T(8,128)}) custom-call(s32[1,2,4,8]{3,2,1,0:T(4,128)} %mask.1, f32[1,2,4,128,1024]{4,3,2,1,0:T(8,128)} %traces.1, f32[1,2,512,512]{3,2,1,0:T(8,128)} %leaf.1), custom_call_target="tpu_custom_call" | custom-call | tf_op jit(solution)/shard_map/pallas_call | solution.py:412
  93.2 1.9 %copy.7 = f32[1,2,256,256]{3,2,1,0:T(8,128)} copy(f32[1,2,256,256]{3,2,1,0:T(8,128)} %get-tuple-element.4) | data formatting | bytes 1048576
  95.1 3.2 %copy.8 = f32[1,2,256,1024]{3,2,1,0:T(8,128)} copy(f32[1,2,256,1024]{3,2,1,0:T(8,128)} %get-tuple-element.5) | data formatting | bytes 4194304

commit v3 on v2

--- a/solution.py
+++ b/solution.py
@@ -111,8 +111,8 @@
 
 def merged(outer_left, outer_right, side, solved):
     across = jnp.transpose(side)
-    ww = outer_left - exact(across[:E], solved[:, :E])
-    low = exact(across[E:], solved)
+    ww = outer_left - near(across[:E], solved[:, :E])
+    low = near(across[E:], solved)
     return ww, -low[:, :E], outer_right - low[:, E:]
 
 
@@ -230,9 +230,6 @@
         for s in (1, 3, 2):
             begin(m1_copy(s, order, y, member(s, False)[2]))
 
-    remote(to.at[1 - x], to.at[1 - x], early_send.at[4], early_recv.at[4], partner).wait_recv()
-    begin(remote(to.at[1 - x], te.at[x], early_send.at[5], early_recv.at[5], inward))
-
     load_traces.wait()
     copy_rx.wait_recv()
     xf = x.astype(F32)
@@ -253,7 +250,7 @@
         if off:
             through.append(rx[outer, :])
             direct.append(placed(rx[face, :], 1.0 - xf))
-        coefficient = 0.5 * (jnp.concatenate(direct, axis=1) - exact(xt, jnp.concatenate(through, axis=1)))
+        coefficient = 0.5 * (jnp.concatenate(direct, axis=1) - near(xt, jnp.concatenate(through, axis=1)))
         high, low = halves(coefficient)
         width = coefficient.shape[1]
         q_hi[row, :, :width] = high
@@ -281,6 +278,8 @@
         partial_load(i)
         for q in (2 * i, 2 * i + 1):
             begin(remote(ps.at[(1 - x) * 4 + q], pr.at[q], pr_send.at[q], pr_recv.at[q], partner))
+    remote(to.at[1 - x], to.at[1 - x], early_send.at[4], early_recv.at[4], partner).wait_recv()
+    begin(remote(to.at[1 - x], te.at[x], early_send.at[5], early_recv.at[5], inward))
     for i in range(2):
         partial_load(2 + i)
 

time: 98.4 us -> 98.4 us (level)
  the two profiles are of different devices: /device:TPU:14 before, /device:TPU:8 now
where the time goes in v3:
time: 98.4 us; the launch traced here: 97 us
  Pallas kernels  91.3 us (93%)
  local copies, waits for them, and re-layouts  5.03 us (5%)
    pallas_call x1, Pallas kernels, body(): pl.pallas_call(functools.partial(kernel, size_x, size_y), out_shape=(jax....  91.3 us
    unnamed x2, local copies, waits for them, and re-layouts  5.03 us

profile of v3, /device:TPU:8, one launch (start us, length us, event | category | flops | bytes accessed | tf_op | source)
XLA Modules:
  0.0 97.0 jit_solution(539304179545585702)
XLA Ops:
  0.6 91.3 %shard_map.50 = (f32[1,2,256,256]{3,2,1,0:T(8,128)}, f32[1,2,256,1024]{3,2,1,0:T(8,128)}) custom-call(s32[1,2,4,8]{3,2,1,0:T(4,128)} %mask.1, f32[1,2,4,128,1024]{4,3,2,1,0:T(8,128)} %traces.1, f32[1,2,512,512]{3,2,1,0:T(8,128)} %leaf.1), custom_call_target="tpu_custom_call" | custom-call | tf_op jit(solution)/shard_map/pallas_call | solution.py:411
  92.0 1.9 %copy.7 = f32[1,2,256,256]{3,2,1,0:T(8,128)} copy(f32[1,2,256,256]{3,2,1,0:T(8,128)} %get-tuple-element.4) | data formatting | bytes 1048576
  93.8 3.2 %copy.8 = f32[1,2,256,1024]{3,2,1,0:T(8,128)} copy(f32[1,2,256,1024]{3,2,1,0:T(8,128)} %get-tuple-element.5) | data formatting | bytes 4194304
